TPU v7x, 32 devices: a whole 2x2x4 slice. The times are simulated.
32 devices in a mesh: groups: 2 (over y), seq: 4 (over z), head: 2 (over x), sub: 2 (over core).
Axes of the slice: x: 2, y: 2, z: 4, core: 2. Of those that a mesh axis runs over, the one named last changes fastest.
Arguments:
- query_rows: bfloat16 [32, 128, 8192], P('head', 'sub', ('groups', 'seq')), parts along dimension 2, may hold values from -6 to 6
- key_rows: bfloat16 [32, 128, 8192], P('head', 'sub', ('groups', 'seq')), parts along dimension 2, may hold values from -0.5 to 0.5
- value_rows: bfloat16 [32, 64, 8192], P('head', None, ('groups', 'seq')), parts along dimension 2, may hold values from -6 to 6
- level_weights: bfloat16 [32, 7, 8192], P('head', None, ('groups', 'seq')), parts along dimension 2, may hold values from 0.29882812 to 3
Outputs:
- mixed_output: bfloat16 [32, 64, 8192], P('head', 'sub', ('groups', 'seq')), parts along dimension 2
There are 2 independent parts, one for each index of `groups`. A program takes and returns all parts, laid end to end along the dimension named above; each array names one. Nothing has to cross between parts.
All inputs are finite; a program needn't handle non-finite values.
Results may differ from a plain program's by a relative error of at most 0.0049.
Values sent between devices are 32-bit elements; how exact they have to be, the bound alone decides.
A program may use at most 128 MiB of HBM per device.

v0:
```python
import functools

import jax
import jax.numpy as jnp
from jax import lax
from jax.experimental import pallas as pl
from jax.experimental.pallas import tpu as pltpu
from jax.sharding import PartitionSpec as P

C = 64
BLOCK = 256
GROUP = 4
F32 = jnp.float32
BF16 = jnp.bfloat16
MESH = pl.DeviceIdType.MESH


def block_bits_of(tokens):
    return (tokens // BLOCK).bit_length() - 1


def local_plan(tokens):
    plan = []
    for b in range(block_bits_of(tokens)):
        for pair in range(tokens // BLOCK >> (b + 1)):
            plan.append((b, pair << (b + 1), 1 << b))
    return plan


def kernel(
    seq_size, q_hbm, k_hbm, v_hbm, w_hbm, out_hbm,
    qb, kb, vb, wb, ob, lst, own, fwd, rbuf, part, rsub,
    in_sem, w_sem, out_sem, send_sem, recv_sem, sub_send, sub_recv,
):
    heads, width, tokens = qb.shape
    groups = heads // GROUP
    blocks = tokens // BLOCK
    bits = seq_size.bit_length() - 1
    stretch_bits = (BLOCK // C).bit_length() - 1
    local_bits = (tokens // C).bit_length() - 1
    plan = local_plan(tokens)
    half = part.shape[1] // 2
    me = lax.axis_index("seq")
    sub = lax.axis_index("sub")

    def in_copy(hbm, buf, kind, g):
        heads_at = pl.ds(g * GROUP, GROUP)
        return pltpu.make_async_copy(hbm.at[heads_at], buf.at[heads_at], in_sem.at[kind, g])

    def out_copy(g):
        heads_at = pl.ds(g * GROUP, GROUP)
        return pltpu.make_async_copy(ob.at[heads_at], out_hbm.at[heads_at], out_sem.at[g])

    def state_copy(g, m, j):
        return pltpu.make_async_remote_copy(
            src_ref=fwd.at[g],
            dst_ref=rbuf.at[m, g],
            send_sem=send_sem.at[g, j],
            recv_sem=recv_sem.at[m, g],
            device_id={"seq": me + 1 + j},
            device_id_type=MESH,
        )

    def sub_copy(g):
        heads_at = pl.ds(g * GROUP, GROUP)
        return pltpu.make_async_remote_copy(
            src_ref=part.at[heads_at, pl.ds(pl.multiple_of((1 - sub) * half, half), half)],
            dst_ref=rsub.at[heads_at],
            send_sem=sub_send.at[g],
            recv_sem=sub_recv.at[g],
            device_id={"sub": 1 - sub},
            device_id_type=MESH,
        )

    barrier = pltpu.get_barrier_semaphore()
    pl.semaphore_signal(barrier, inc=1, device_id={"sub": 1 - sub}, device_id_type=MESH)
    for d in range(1, seq_size):
        pl.semaphore_signal(
            barrier, inc=1, device_id={"seq": lax.rem(me + d, seq_size)}, device_id_type=MESH
        )
    for g in range(groups):
        in_copy(k_hbm, kb, 0, g).start()
        in_copy(v_hbm, vb, 1, g).start()
    w_copy = pltpu.make_async_copy(w_hbm, wb, w_sem)
    w_copy.start()
    for g in range(groups):
        in_copy(q_hbm, qb, 2, g).start()

    lane = lax.broadcasted_iota(jnp.int32, (width, 128), 1)
    low = lane < 64
    low_f = low.astype(F32)
    low_b = low_f.astype(BF16)
    high_b = (1.0 - low_f).astype(BF16)

    def block_diag(x):
        zero = jnp.zeros((width, 128), BF16)
        rows = []
        for t in range(2):
            tile = x[:, t * 128:(t + 1) * 128]
            for mask in (low_b, high_b):
                pair = [zero, zero]
                pair[t] = tile * mask
                rows.append(jnp.concatenate(pair, axis=1))
        return jnp.concatenate(rows, axis=0)

    def states(g):
        in_copy(k_hbm, kb, 0, g).wait()
        in_copy(v_hbm, vb, 1, g).wait()
        packed = []
        for i in range(blocks):
            at = slice(i * BLOCK, (i + 1) * BLOCK)
            tiles = []
            for t in range(2):
                pair_at = pl.ds(g * GROUP + 2 * t, 2)
                values = vb[pair_at, :, at].reshape(128, BLOCK)
                keys = kb[pair_at, :, at].reshape(128, BLOCK)
                both = lax.dot_general(
                    values, keys, (((1,), (1,)), ((), ())), preferred_element_type=F32
                )
                tiles.append(jnp.where(low, both[:64], both[64:]))
            packed.append(jnp.concatenate(tiles, axis=1))
        for at, (_, first, count) in enumerate(plan):
            lst[g, at] = functools.reduce(jnp.add, packed[first:first + count]).astype(BF16)
        own[g] = functools.reduce(jnp.add, packed)

    def forward(g):
        for m in range(bits):
            @pl.when(lax.rem(me, 2 << m) == (1 << m) - 1)
            def _():
                total = own[g]
                for l in range(m):
                    state_copy(g, l, 0).wait_recv()
                    total = total + rbuf[l, g]
                fwd[g] = total
                for j in reversed(range(1 << m)):
                    state_copy(g, m, j).start()

    def forward_first(g):
        @pl.when(lax.rem(me, 2) == 0)
        def _():
            fwd[g] = own[g]
            state_copy(g, 0, 0).start()

    def forward_later(g):
        for m in range(1, bits):
            @pl.when(lax.rem(me, 2 << m) == (1 << m) - 1)
            def _():
                total = own[g]
                for l in range(m):
                    state_copy(g, l, 0).wait_recv()
                    total = total + rbuf[l, g]
                fwd[g] = total
                for j in reversed(range(1 << m)):
                    state_copy(g, m, j).start()

    def factor_row(weights, b):
        return weights[b + 1:b + 2] * (2 ** b * C) ** (-0.5)

    col = lax.broadcasted_iota(jnp.int32, (C, 128), 1)
    row = lax.broadcasted_iota(jnp.int32, (C, 128), 0)
    causal = (col >= row, col >= row + C)
    col_row = lax.broadcasted_iota(jnp.int32, (1, 128), 1) < C

    def local(g):
        in_copy(q_hbm, qb, 2, g).wait()
        for i in range(blocks):
            at = slice(i * BLOCK, (i + 1) * BLOCK)
            levels = [
                (s, b) for s, (b, first, count) in enumerate(plan)
                if i >> b & 1 and (i >> (b + 1)) << (b + 1) == first
            ]
            if levels:
                queries = qb[pl.ds(g * GROUP, GROUP), :, at].reshape(GROUP * width, BLOCK)
                lhs = jnp.concatenate([block_diag(lst[g, s]) for s, _ in levels], axis=0)
                reads = jnp.dot(lhs, queries, preferred_element_type=F32)
            for h in range(GROUP):
                head = g * GROUP + h
                weights = wb[head, :, at].astype(F32)
                scores = lax.dot_general(
                    kb[head, :, at], qb[head, :, at], (((0,), (0,)), ((), ())),
                    preferred_element_type=F32,
                )
                diag = weights[0:1] * C ** (-0.5)
                one = factor_row(weights, 0)
                two = factor_row(weights, 1)
                rows = []
                for c in range(BLOCK // C):
                    t = c // 2
                    near = slice(t * 128, (t + 1) * 128)
                    if c % 2 == 0:
                        mult = jnp.where(col_row, diag[:, near], one[:, near])
                    else:
                        mult = diag[:, near]
                    part_rows = scores[c * C:(c + 1) * C]
                    tile = jnp.where(causal[c % 2], part_rows[:, near] * mult, 0.0).astype(BF16)
                    if t == 0:
                        pair = [tile, (part_rows[:, 128:] * two[:, 128:]).astype(BF16)]
                    else:
                        pair = [jnp.zeros((C, 128), BF16), tile]
                    rows.append(jnp.concatenate(pair, axis=1))
                masked = jnp.concatenate(rows, axis=0)
                total = jnp.dot(vb[head, :, at], masked, preferred_element_type=F32)
                for n, (_, b) in enumerate(levels):
                    base = n * GROUP * 64 + h * 64
                    total = total + reads[base:base + 64] * factor_row(weights, b + stretch_bits)
                part[head, :, at] = total

    def far(g, m):
        @pl.when(lax.rem(me // (1 << m), 2) == 1)
        def _():
            waited = jnp.logical_and(
                lax.rem(me, 2 << m) == (2 << m) - 1, me != seq_size - 1
            )

            @pl.when(jnp.logical_not(waited))
            def _():
                state_copy(g, m, 0).wait_recv()

            lhs = block_diag(rbuf[m, g].astype(BF16))
            for i in range(blocks):
                at = slice(i * BLOCK, (i + 1) * BLOCK)
                queries = qb[pl.ds(g * GROUP, GROUP), :, at].reshape(GROUP * width, BLOCK)
                reads = jnp.dot(lhs, queries, preferred_element_type=F32)
                for h in range(GROUP):
                    head = g * GROUP + h
                    weights = wb[head, :, at].astype(F32)
                    part[head, :, at] += reads[h * 64:(h + 1) * 64] * factor_row(
                        weights, local_bits + m
                    )

    def finish(g):
        sub_copy(g).wait_recv()
        heads_at = pl.ds(g * GROUP, GROUP)
        mine = part[heads_at, pl.ds(pl.multiple_of(sub * half, half), half), :]
        ob[heads_at] = (mine + rsub[heads_at]).astype(BF16)
        out_copy(g).start()

    def loop(body):
        lax.fori_loop(0, groups, lambda g, carry: (body(g), carry)[1], 0)

    states(0)
    pl.semaphore_wait(barrier, seq_size)
    forward_first(0)

    @pl.loop(1, groups)
    def _(g):
        states(g)
        forward_first(g)

    w_copy.wait()

    @pl.loop(0, groups)
    def _(g):
        forward_later(g)
        local(g)

    for m in range(bits - 1):
        @pl.loop(0, groups)
        def _(g):
            far(g, m)

    @pl.loop(0, groups)
    def _(g):
        far(g, bits - 1)
        sub_copy(g).start()

        @pl.when(g > 0)
        def _():
            finish(g - 1)

    finish(groups - 1)

    @pl.loop(0, groups)
    def _(g):
        sub_copy(g).wait_send()
        out_copy(g).wait()
        for m in range(bits):
            @pl.when(lax.rem(me, 2 << m) == (1 << m) - 1)
            def _():
                for j in range(1 << m):
                    state_copy(g, m, j).wait_send()


def on_device(seq_size, query_rows, key_rows, value_rows, level_weights):
    heads, width, tokens = query_rows.shape
    value_width = value_rows.shape[1]
    groups = heads // GROUP
    bits = seq_size.bit_length() - 1
    packed = (value_width, GROUP * width)
    hbm = pl.BlockSpec(memory_space=pl.ANY)
    return pl.pallas_call(
        functools.partial(kernel, seq_size),
        out_shape=jax.ShapeDtypeStruct((heads, value_width // 2, tokens), BF16),
        in_specs=[hbm] * 4,
        out_specs=hbm,
        scratch_shapes=[
            pltpu.VMEM(query_rows.shape, BF16),
            pltpu.VMEM(key_rows.shape, BF16),
            pltpu.VMEM(value_rows.shape, BF16),
            pltpu.VMEM(level_weights.shape, BF16),
            pltpu.VMEM((heads, value_width // 2, tokens), BF16),
            pltpu.VMEM((groups, len(local_plan(tokens))) + packed, BF16),
            pltpu.VMEM((groups,) + packed, F32),
            pltpu.VMEM((groups,) + packed, F32),
            pltpu.VMEM((bits, groups) + packed, F32),
            pltpu.VMEM((heads, value_width, tokens), F32),
            pltpu.VMEM((heads, value_width // 2, tokens), F32),
            pltpu.SemaphoreType.DMA((3, groups)),
            pltpu.SemaphoreType.DMA,
            pltpu.SemaphoreType.DMA((groups,)),
            pltpu.SemaphoreType.DMA((groups, seq_size // 2)),
            pltpu.SemaphoreType.DMA((bits, groups)),
            pltpu.SemaphoreType.DMA((groups,)),
            pltpu.SemaphoreType.DMA((groups,)),
        ],
        compiler_params=pltpu.CompilerParams(
            collective_id=0, has_side_effects=True, vmem_limit_bytes=56 * 2**20
        ),
    )(query_rows, key_rows, value_rows, level_weights)


def solution(mesh):
    placed = (
        P("head", "sub", ("groups", "seq")),
        P("head", "sub", ("groups", "seq")),
        P("head", None, ("groups", "seq")),
        P("head", None, ("groups", "seq")),
    )
    return jax.shard_map(
        functools.partial(on_device, mesh.shape["seq"]),
        mesh=mesh,
        in_specs=placed,
        out_specs=P("head", "sub", ("groups", "seq")),
        check_vma=False,
    )
```

profile of v0, /device:TPU:15, one launch (start us, length us, event | category | flops | bytes accessed | tf_op | source)
XLA Modules:
  0.0 28.9 jit_solution(12131051620191326230)
XLA Ops:
  0.0 1.8 %copy.5.w_hbm = bf16[16,7,1024]{2,1,0:T(8,128)(2,1)} copy(bf16[16,7,1024]{2,0,1:T(8,128)(2,1)} %param.7) | data formatting | bytes 458752 | tf_op args[3]
  1.8 24.8 %shard_map.46 = bf16[16,32,1024]{2,1,0:T(8,128)(2,1)} custom-call(bf16[16,64,1024]{2,1,0:T(8,128)(2,1)} %q_hbm.1, bf16[16,64,1024]{2,1,0:T(8,128)(2,1)} %k_hbm.1, bf16[16,64,1024]{2,1,0:T(8,128)(2,1)} %v_hbm.1, bf16[16,7,1024]{2,1,0:T(8,128)(2,1)} %copy.5.w_hbm), custom_call_target="tpu_custom_call" | custom-call | tf_op jit(solution)/shard_map/pallas_call | solution.py:291
  26.6 2.3 %copy.7 = bf16[16,32,1024]{2,1,0:T(8,128)(2,1)} copy(bf16[16,32,1024]{2,1,0:T(8,128)(2,1)} %shard_map.46) | data formatting | bytes 2097152
where the time goes:
time: 29.1 us; the launch traced here: 28.9 us
  Pallas kernels  24.8 us (85%)
  local copies, waits for them, and re-layouts  4.06 us (14%)
    pallas_call x1, Pallas kernels, on_device(): pl.pallas_call(functools.partial(kernel, seq_size), out_shape=jax.ShapeDt...  24.8 us
    unnamed x2, local copies, waits for them, and re-layouts  4.06 us

commit v1 on v0

--- a/solution.py
+++ b/solution.py
@@ -29,7 +29,7 @@
 
 def kernel(
     seq_size, q_hbm, k_hbm, v_hbm, w_hbm, out_hbm,
-    qb, kb, vb, wb, ob, lst, own, fwd, rbuf, part, rsub,
+    qb, kb, vb, wb, wf, ob, lst, own, fwd, rbuf, part, rsub,
     in_sem, w_sem, out_sem, send_sem, recv_sem, sub_send, sub_recv,
 ):
     heads, width, tokens = qb.shape
@@ -123,18 +123,6 @@
             lst[g, at] = functools.reduce(jnp.add, packed[first:first + count]).astype(BF16)
         own[g] = functools.reduce(jnp.add, packed)
 
-    def forward(g):
-        for m in range(bits):
-            @pl.when(lax.rem(me, 2 << m) == (1 << m) - 1)
-            def _():
-                total = own[g]
-                for l in range(m):
-                    state_copy(g, l, 0).wait_recv()
-                    total = total + rbuf[l, g]
-                fwd[g] = total
-                for j in reversed(range(1 << m)):
-                    state_copy(g, m, j).start()
-
     def forward_first(g):
         @pl.when(lax.rem(me, 2) == 0)
         def _():
@@ -153,8 +141,8 @@
                 for j in reversed(range(1 << m)):
                     state_copy(g, m, j).start()
 
-    def factor_row(weights, b):
-        return weights[b + 1:b + 2] * (2 ** b * C) ** (-0.5)
+    def factor_row(head, level, at):
+        return wf[level, pl.ds(head, 1), at]
 
     col = lax.broadcasted_iota(jnp.int32, (C, 128), 1)
     row = lax.broadcasted_iota(jnp.int32, (C, 128), 0)
@@ -175,14 +163,11 @@
                 reads = jnp.dot(lhs, queries, preferred_element_type=F32)
             for h in range(GROUP):
                 head = g * GROUP + h
-                weights = wb[head, :, at].astype(F32)
                 scores = lax.dot_general(
                     kb[head, :, at], qb[head, :, at], (((0,), (0,)), ((), ())),
                     preferred_element_type=F32,
                 )
-                diag = weights[0:1] * C ** (-0.5)
-                one = factor_row(weights, 0)
-                two = factor_row(weights, 1)
+                diag, one, two = (factor_row(head, n, at) for n in range(3))
                 rows = []
                 for c in range(BLOCK // C):
                     t = c // 2
@@ -202,7 +187,9 @@
                 total = jnp.dot(vb[head, :, at], masked, preferred_element_type=F32)
                 for n, (_, b) in enumerate(levels):
                     base = n * GROUP * 64 + h * 64
-                    total = total + reads[base:base + 64] * factor_row(weights, b + stretch_bits)
+                    total = total + reads[base:base + 64] * factor_row(
+                        head, b + stretch_bits + 1, at
+                    )
                 part[head, :, at] = total
 
     def far(g, m):
@@ -223,9 +210,8 @@
                 reads = jnp.dot(lhs, queries, preferred_element_type=F32)
                 for h in range(GROUP):
                     head = g * GROUP + h
-                    weights = wb[head, :, at].astype(F32)
                     part[head, :, at] += reads[h * 64:(h + 1) * 64] * factor_row(
-                        weights, local_bits + m
+                        head, local_bits + m + 1, at
                     )
 
     def finish(g):
@@ -248,26 +234,31 @@
         forward_first(g)
 
     w_copy.wait()
+    wf[0] = wb[0].astype(F32) * C ** (-0.5)
+    for b in range(local_bits + bits):
+        wf[b + 1] = wb[b + 1].astype(F32) * (2 ** b * C) ** (-0.5)
+
+    def send(g):
+        for m in range(bits):
+            far(g, m)
+        sub_copy(g).start()
 
     @pl.loop(0, groups)
     def _(g):
+        local(g)
         forward_later(g)
-        local(g)
-
-    for m in range(bits - 1):
-        @pl.loop(0, groups)
-        def _(g):
-            far(g, m)
-
-    @pl.loop(0, groups)
-    def _(g):
-        far(g, bits - 1)
-        sub_copy(g).start()
 
         @pl.when(g > 0)
         def _():
-            finish(g - 1)
-
+            send(g - 1)
+
+        @pl.when(g > 1)
+        def _():
+            finish(g - 2)
+
+    send(groups - 1)
+    if groups > 1:
+        finish(groups - 2)
     finish(groups - 1)
 
     @pl.loop(0, groups)
@@ -284,10 +275,11 @@
 def on_device(seq_size, query_rows, key_rows, value_rows, level_weights):
     heads, width, tokens = query_rows.shape
     value_width = value_rows.shape[1]
+    weights = jnp.swapaxes(level_weights, 0, 1)
     groups = heads // GROUP
     bits = seq_size.bit_length() - 1
     packed = (value_width, GROUP * width)
-    hbm = pl.BlockSpec(memory_space=pl.ANY)
+    hbm = pl.BlockSpec(memory_space=pltpu.HBM)
     return pl.pallas_call(
         functools.partial(kernel, seq_size),
         out_shape=jax.ShapeDtypeStruct((heads, value_width // 2, tokens), BF16),
@@ -297,7 +289,8 @@
             pltpu.VMEM(query_rows.shape, BF16),
             pltpu.VMEM(key_rows.shape, BF16),
             pltpu.VMEM(value_rows.shape, BF16),
-            pltpu.VMEM(level_weights.shape, BF16),
+            pltpu.VMEM(weights.shape, BF16),
+            pltpu.VMEM(weights.shape, F32),
             pltpu.VMEM((heads, value_width // 2, tokens), BF16),
             pltpu.VMEM((groups, len(local_plan(tokens))) + packed, BF16),
             pltpu.VMEM((groups,) + packed, F32),
@@ -316,7 +309,7 @@
         compiler_params=pltpu.CompilerParams(
             collective_id=0, has_side_effects=True, vmem_limit_bytes=56 * 2**20
         ),
-    )(query_rows, key_rows, value_rows, level_weights)
+    )(query_rows, key_rows, value_rows, weights)
 
 
 def solution(mesh):

time: 29.1 us -> 25.4 us (0.87)
  the two profiles are of different devices: /device:TPU:15 before, /device:TPU:17 now
where the time goes in v1:
time: 25.4 us; the launch traced here: 25.2 us
  Pallas kernels  22.9 us (90%)
  local copies, waits for them, and re-layouts  2.29 us (9%)
    pallas_call x1, Pallas kernels, on_device(): pl.pallas_call(functools.partial(kernel, seq_size), out_shape=jax.ShapeDt...  22.9 us
    unnamed x1, local copies, waits for them, and re-layouts  2.29 us

profile of v1, /device:TPU:17, one launch (start us, length us, event | category | flops | bytes accessed | tf_op | source)
XLA Modules:
  0.0 25.2 jit_solution(1142892108397044964)
XLA Ops:
  0.0 22.9 %shard_map.46 = bf16[16,32,1024]{2,1,0:T(8,128)(2,1)} custom-call(bf16[16,64,1024]{2,1,0:T(8,128)(2,1)} %q_hbm.1, bf16[16,64,1024]{2,1,0:T(8,128)(2,1)} %k_hbm.1, bf16[16,64,1024]{2,1,0:T(8,128)(2,1)} %v_hbm.1, bf16[7,16,1024]{2,1,0:T(8,128)(2,1)} %bitcast.1), custom_call_target="tpu_custom_call" | custom-call | tf_op jit(solution)/shard_map/pallas_call | solution.py:283
  23.0 2.3 %copy.6 = bf16[16,32,1024]{2,1,0:T(8,128)(2,1)} copy(bf16[16,32,1024]{2,1,0:T(8,128)(2,1)} %shard_map.46) | data formatting | bytes 2097152

commit v2 on v1

--- a/solution.py
+++ b/solution.py
@@ -161,6 +161,7 @@
                 queries = qb[pl.ds(g * GROUP, GROUP), :, at].reshape(GROUP * width, BLOCK)
                 lhs = jnp.concatenate([block_diag(lst[g, s]) for s, _ in levels], axis=0)
                 reads = jnp.dot(lhs, queries, preferred_element_type=F32)
+            grid = []
             for h in range(GROUP):
                 head = g * GROUP + h
                 scores = lax.dot_general(
@@ -183,8 +184,10 @@
                     else:
                         pair = [jnp.zeros((C, 128), BF16), tile]
                     rows.append(jnp.concatenate(pair, axis=1))
-                masked = jnp.concatenate(rows, axis=0)
-                total = jnp.dot(vb[head, :, at], masked, preferred_element_type=F32)
+                grid.append(jnp.concatenate(rows, axis=0))
+            for h in range(GROUP):
+                head = g * GROUP + h
+                total = jnp.dot(vb[head, :, at], grid[h], preferred_element_type=F32)
                 for n, (_, b) in enumerate(levels):
                     base = n * GROUP * 64 + h * 64
                     total = total + reads[base:base + 64] * factor_row(

time: 25.4 us -> 23.6 us (0.929)
  Pallas kernels: 22.9 us -> 21.2 us
    pallas_call x1, Pallas kernels: 22.9 us -> 21.2 us  [on_device(): pl.pallas_call(functools.partial(kernel, seq_size), out_shape=jax.ShapeDt...]
where the time goes in v2:
time: 23.6 us; the launch traced here: 23.5 us
  Pallas kernels  21.2 us (90%)
  local copies, waits for them, and re-layouts  2.29 us (10%)
    pallas_call x1, Pallas kernels, on_device(): pl.pallas_call(functools.partial(kernel, seq_size), out_shape=jax.ShapeDt...  21.2 us
    unnamed x1, local copies, waits for them, and re-layouts  2.29 us

profile of v2, /device:TPU:17, one launch (start us, length us, event | category | flops | bytes accessed | tf_op | source)
XLA Modules:
  0.0 23.5 jit_solution(882101827550457508)
XLA Ops:
  0.0 21.2 %shard_map.46 = bf16[16,32,1024]{2,1,0:T(8,128)(2,1)} custom-call(bf16[16,64,1024]{2,1,0:T(8,128)(2,1)} %q_hbm.1, bf16[16,64,1024]{2,1,0:T(8,128)(2,1)} %k_hbm.1, bf16[16,64,1024]{2,1,0:T(8,128)(2,1)} %v_hbm.1, bf16[7,16,1024]{2,1,0:T(8,128)(2,1)} %bitcast.1), custom_call_target="tpu_custom_call" | custom-call | tf_op jit(solution)/shard_map/pallas_call | solution.py:286
  21.2 2.3 %copy.6 = bf16[16,32,1024]{2,1,0:T(8,128)(2,1)} copy(bf16[16,32,1024]{2,1,0:T(8,128)(2,1)} %shard_map.46) | data formatting | bytes 2097152

commit v3 on v2

--- a/solution.py
+++ b/solution.py
@@ -287,7 +287,7 @@
         functools.partial(kernel, seq_size),
         out_shape=jax.ShapeDtypeStruct((heads, value_width // 2, tokens), BF16),
         in_specs=[hbm] * 4,
-        out_specs=hbm,
+        out_specs=pl.BlockSpec(memory_space=pl.ANY),
         scratch_shapes=[
             pltpu.VMEM(query_rows.shape, BF16),
             pltpu.VMEM(key_rows.shape, BF16),
@@ -310,7 +310,7 @@
             pltpu.SemaphoreType.DMA((groups,)),
         ],
         compiler_params=pltpu.CompilerParams(
-            collective_id=0, has_side_effects=True, vmem_limit_bytes=56 * 2**20
+            collective_id=0, has_side_effects=True, vmem_limit_bytes=52 * 2**20
         ),
     )(query_rows, key_rows, value_rows, weights)
 

time: 23.6 us -> 22.6 us (0.958)
  Pallas kernels: 21.2 us -> 20.5 us
  local copies, waits for them, and re-layouts: 2.29 us -> 1.91 us
    pallas_call x1, Pallas kernels: 21.2 us -> 20.5 us  [on_device(): pl.pallas_call(functools.partial(kernel, seq_size), out_shape=jax.ShapeDt...]
    unnamed x1 -> x3, local copies, waits for them, and re-layouts: 2.29 us -> 1.91 us
where the time goes in v3:
time: 22.6 us; the launch traced here: 22.5 us
  Pallas kernels  20.5 us (91%)
  local copies, waits for them, and re-layouts  1.91 us (8%)
    pallas_call x1, Pallas kernels, on_device(): pl.pallas_call(functools.partial(kernel, seq_size), out_shape=jax.ShapeDt...  20.5 us
    unnamed x3, local copies, waits for them, and re-layouts  1.91 us

profile of v3, /device:TPU:17, one launch (start us, length us, event | category | flops | bytes accessed | tf_op | source)
XLA Modules:
  0.0 22.5 jit_solution(1519811249543721609)
XLA Ops:
  0.0 0.0 copy-start
  0.0 0.9 %copy-done = bf16[16,7,1024]{2,0,1:T(8,128)(2,1)S(1)} copy-done((bf16[16,7,1024]{2,0,1:T(8,128)(2,1)S(1)}, bf16[16,7,1024]{2,0,1:T(8,128)(2,1)}, u32[]{:S(2)}) %copy-start) | copy-done | bytes 229400
  0.9 20.5 %shard_map.46 = bf16[16,32,1024]{2,1,0:T(8,128)(2,1)S(1)} custom-call(bf16[16,64,1024]{2,1,0:T(8,128)(2,1)} %q_hbm.1, bf16[16,64,1024]{2,1,0:T(8,128)(2,1)} %k_hbm.1, bf16[16,64,1024]{2,1,0:T(8,128)(2,1)} %v_hbm.1, bf16[7,16,1024]{2,1,0:T(8,128)(2,1)S(1)} %bitcast.1), custom_call_target="tpu_custom_call" | custom-call | tf_op jit(solution)/shard_map/pallas_call | solution.py:286
  21.5 1.0 %copy.6 = bf16[16,32,1024]{2,1,0:T(8,128)(2,1)} copy(bf16[16,32,1024]{2,1,0:T(8,128)(2,1)S(1)} %shard_map.46) | data formatting | bytes 2097152
Async XLA Ops:
  0.0 0.9 %copy-start = (bf16[16,7,1024]{2,0,1:T(8,128)(2,1)S(1)}, bf16[16,7,1024]{2,0,1:T(8,128)(2,1)}, u32[]{:S(2)}) copy-start(bf16[16,7,1024]{2,0,1:T(8,128)(2,1)} %param.7) | copy-start | bytes 688132

commit v4 on v3

--- a/solution.py
+++ b/solution.py
@@ -28,9 +28,9 @@
 
 
 def kernel(
-    seq_size, q_hbm, k_hbm, v_hbm, w_hbm, out_hbm,
-    qb, kb, vb, wb, wf, ob, lst, own, fwd, rbuf, part, rsub,
-    in_sem, w_sem, out_sem, send_sem, recv_sem, sub_send, sub_recv,
+    seq_size, q_hbm, k_hbm, v_hbm, w_hbm, out,
+    qb, kb, vb, wb, wf, lst, own, fwd, rbuf, part, rsub,
+    in_sem, w_sem, send_sem, recv_sem, sub_send, sub_recv,
 ):
     heads, width, tokens = qb.shape
     groups = heads // GROUP
@@ -46,10 +46,6 @@
     def in_copy(hbm, buf, kind, g):
         heads_at = pl.ds(g * GROUP, GROUP)
         return pltpu.make_async_copy(hbm.at[heads_at], buf.at[heads_at], in_sem.at[kind, g])
-
-    def out_copy(g):
-        heads_at = pl.ds(g * GROUP, GROUP)
-        return pltpu.make_async_copy(ob.at[heads_at], out_hbm.at[heads_at], out_sem.at[g])
 
     def state_copy(g, m, j):
         return pltpu.make_async_remote_copy(
@@ -221,8 +217,7 @@
         sub_copy(g).wait_recv()
         heads_at = pl.ds(g * GROUP, GROUP)
         mine = part[heads_at, pl.ds(pl.multiple_of(sub * half, half), half), :]
-        ob[heads_at] = (mine + rsub[heads_at]).astype(BF16)
-        out_copy(g).start()
+        out[heads_at] = (mine + rsub[heads_at]).astype(BF16)
 
     def loop(body):
         lax.fori_loop(0, groups, lambda g, carry: (body(g), carry)[1], 0)
@@ -267,7 +262,6 @@
     @pl.loop(0, groups)
     def _(g):
         sub_copy(g).wait_send()
-        out_copy(g).wait()
         for m in range(bits):
             @pl.when(lax.rem(me, 2 << m) == (1 << m) - 1)
             def _():
@@ -287,14 +281,13 @@
         functools.partial(kernel, seq_size),
         out_shape=jax.ShapeDtypeStruct((heads, value_width // 2, tokens), BF16),
         in_specs=[hbm] * 4,
-        out_specs=pl.BlockSpec(memory_space=pl.ANY),
+        out_specs=pl.BlockSpec(memory_space=pltpu.VMEM),
         scratch_shapes=[
             pltpu.VMEM(query_rows.shape, BF16),
             pltpu.VMEM(key_rows.shape, BF16),
             pltpu.VMEM(value_rows.shape, BF16),
             pltpu.VMEM(weights.shape, BF16),
             pltpu.VMEM(weights.shape, F32),
-            pltpu.VMEM((heads, value_width // 2, tokens), BF16),
             pltpu.VMEM((groups, len(local_plan(tokens))) + packed, BF16),
             pltpu.VMEM((groups,) + packed, F32),
             pltpu.VMEM((groups,) + packed, F32),
@@ -303,7 +296,6 @@
             pltpu.VMEM((heads, value_width // 2, tokens), F32),
             pltpu.SemaphoreType.DMA((3, groups)),
             pltpu.SemaphoreType.DMA,
-            pltpu.SemaphoreType.DMA((groups,)),
             pltpu.SemaphoreType.DMA((groups, seq_size // 2)),
             pltpu.SemaphoreType.DMA((bits, groups)),
             pltpu.SemaphoreType.DMA((groups,)),

time: 22.6 us -> 22.5 us (level)
  no operation moved by 1% of the time
where the time goes in v4:
time: 22.5 us; the launch traced here: 22.4 us
  Pallas kernels  20.5 us (91%)
  local copies, waits for them, and re-layouts  1.91 us (8%)
    pallas_call x1, Pallas kernels, on_device(): pl.pallas_call(functools.partial(kernel, seq_size), out_shape=jax.ShapeDt...  20.5 us
    unnamed x3, local copies, waits for them, and re-layouts  1.91 us

profile of v4, /device:TPU:17, one launch (start us, length us, event | category | flops | bytes accessed | tf_op | source)
XLA Modules:
  0.0 22.4 jit_solution(11690521277420762258)
XLA Ops:
  0.0 0.0 copy-start
  0.0 0.9 %copy-done = bf16[16,7,1024]{2,0,1:T(8,128)(2,1)S(1)} copy-done((bf16[16,7,1024]{2,0,1:T(8,128)(2,1)S(1)}, bf16[16,7,1024]{2,0,1:T(8,128)(2,1)}, u32[]{:S(2)}) %copy-start) | copy-done | bytes 229400
  0.9 20.5 %shard_map.46 = bf16[16,32,1024]{2,1,0:T(8,128)(2,1)S(1)} custom-call(bf16[16,64,1024]{2,1,0:T(8,128)(2,1)} %q_hbm.1, bf16[16,64,1024]{2,1,0:T(8,128)(2,1)} %k_hbm.1, bf16[16,64,1024]{2,1,0:T(8,128)(2,1)} %v_hbm.1, bf16[7,16,1024]{2,1,0:T(8,128)(2,1)S(1)} %bitcast.1), custom_call_target="tpu_custom_call" | custom-call | tf_op jit(solution)/shard_map/pallas_call | solution.py:280
  21.4 1.0 %copy.6 = bf16[16,32,1024]{2,1,0:T(8,128)(2,1)} copy(bf16[16,32,1024]{2,1,0:T(8,128)(2,1)S(1)} %shard_map.46) | data formatting | bytes 2097152
Async XLA Ops:
  0.0 0.9 %copy-start = (bf16[16,7,1024]{2,0,1:T(8,128)(2,1)S(1)}, bf16[16,7,1024]{2,0,1:T(8,128)(2,1)}, u32[]{:S(2)}) copy-start(bf16[16,7,1024]{2,0,1:T(8,128)(2,1)} %param.7) | copy-start | bytes 688132
